TPU v7x, 512 devices: a whole 4x8x8 slice. The times are simulated.
512 devices in a mesh: grp: 8 (over x, core), seq: 64 (over z, y).
Axes of the slice: x: 4, y: 8, z: 8, core: 2. Of those that a mesh axis runs over, the one named last changes fastest.
Arguments:
- llm_grad: bfloat16 [16384, 8192], P('seq', 'grp'), may hold values from -6 to 6
- image_grid: int32 [4096, 2], replicated, may hold values from 1 to 3, as said below
- image_owner: int32 [4096], replicated, may hold values from 0 to 63, as said below
- row_start: int32 [4096], replicated, may hold values from 0 to 255, as said below
- merger_pre: bfloat16 [192, 64, 2560], P(None, 'seq', 'grp'), may hold values from -6 to 6
- vit_out: bfloat16 [768, 64, 1280], P(None, 'seq'), may hold values from -6 to 6
- vit_pre: bfloat16 [768, 64, 2560], P(None, 'seq', 'grp'), may hold values from -6 to 6
- ln_gain: float32 [1280], replicated, may hold values from 0.25 to 1.75
- merger_out_w: bfloat16 [8192, 2560], P('seq', 'grp'), may hold values from -0.0625 to 0.0625
- merger_in_w: bfloat16 [2560, 5120], P('grp', 'seq'), may hold values from -0.125 to 0.125
- vit_fc2_w: bfloat16 [1280, 2560], P('seq', 'grp'), may hold values from -0.15625 to 0.15625
Outputs:
- patch_grad: bfloat16 [768, 64, 1280], P('grp', 'seq')
- fc1_grad: bfloat16 [768, 64, 2560], P(None, 'seq', 'grp')
- fc2_w_grad: float32 [1280, 2560], P('seq', 'grp')
Inputs may be any that keep to these rules, and one draw needn't show every extreme that they name: `image_grid`: height times width is 1 to 3; the first image of every shard is 1 by 3; the last image of shard 0 is 1 by 1. `image_owner`: the 64 images of one shard have 64 different owners. An image's rows row_start to row_start + t - 1 lie inside its shard and meet no other image's rows; a shard's images follow the order of k; the last image of every shard ends at the shard's last row; the first image of shard 0 starts at row 0.
All inputs are finite; a program needn't handle non-finite values.
Results may differ from a plain program's by a relative error of at most 0.02.
Values may be sent and summed in bfloat16 or wider, within the bound.
No kernel may reach another device: no remote copies, remote signals or barrier semaphores. Data moves between devices by JAX's collectives and lax.ppermute only.
A program may use at most 64 MiB of HBM per device.

v0:
```python
import jax
import jax.numpy as jnp
from jax import lax
from jax.sharding import Mesh
from jax.sharding import PartitionSpec as P

SLOT = 3
SEQ = ("seq_0", "seq_1")


def joined_along(tiles, dim):
    tiles = jnp.moveaxis(tiles, 0, dim)
    lengths = tiles.shape
    return tiles.reshape(*lengths[:dim], lengths[dim] * lengths[dim + 1], *lengths[dim + 2 :])


def gather_in_order(value, axes, order):
    tiles = value[None]
    for k in order:
        tiles = lax.all_gather(tiles, axes[k], axis=0, tiled=True)
    current = [lax.axis_size(axes[k]) for k in reversed(order)]
    tiles = tiles.reshape(*current, *value.shape)
    turned = sorted(range(len(order)), key=lambda place: order[len(order) - 1 - place])
    return tiles.transpose(*turned, *range(len(order), tiles.ndim)).reshape(-1, *value.shape)


def gather_axes(value, axes, order, dim):
    return joined_along(gather_in_order(value, axes, order), dim)


def filled_up(lines, size):
    spare = -lines.shape[0] % size
    if not spare:
        return lines
    return jnp.concatenate([lines, jnp.zeros((spare, *lines.shape[1:]), lines.dtype)])


def sum_by_parts(value, axis):
    lines = value.reshape(-1, *value.shape[1:][-1:])
    own = lax.psum_scatter(
        filled_up(lines, lax.axis_size(axis)), axis, scatter_dimension=0, tiled=True
    )
    whole = lax.all_gather(own, axis).reshape(-1, *lines.shape[1:])
    return lax.slice_in_dim(whole, 0, len(lines)).reshape(value.shape)


def copy_for_each(value, axis):
    copies = jnp.broadcast_to(value, (lax.axis_size(axis), *value.shape))
    return lax.all_to_all(copies, axis, split_axis=0, concat_axis=0, tiled=True)


def gather_directly(value, axis, dim):
    return joined_along(copy_for_each(value, axis), dim)


def in_blocks(value, dim, size):
    lengths = value.shape
    tiles = value.reshape(*lengths[:dim], size, lengths[dim] // size, *lengths[dim + 1 :])
    return jnp.moveaxis(tiles, dim, 0)


def sum_at_owner(value, axis, dim):
    tiles = in_blocks(value, dim, lax.axis_size(axis))
    arrived = lax.all_to_all(tiles, axis, split_axis=0, concat_axis=0, tiled=True)
    return arrived.astype(jnp.float32).sum(axis=0)


def gelu_slope(values):
    return (
        0.5 * (1.0 + lax.erf(values * 0.7071067811865476))
        + values * jnp.exp(-0.5 * values * values) * 0.3989422804014327
    )


def patch_table(widths, counts, slots):
    places = jnp.arange(4 * slots, dtype=jnp.int32)
    merged = places // 4
    corner = places % 4
    row_in = merged[None, :] // widths[:, None]
    col_in = merged[None, :] % widths[:, None]
    target = (
        (2 * row_in + corner[None, :] // 2) * (2 * widths[:, None])
        + 2 * col_in
        + corner[None, :] % 2
    )
    usable = merged[None, :] < counts[:, None]
    return ((target[:, None, :] == places[None, :, None]) & usable[:, None, :]).astype(jnp.float32)


def norm_backward(upstream, inputs, scales):
    average = jnp.mean(inputs, -1, keepdims=True)
    centred = inputs - average
    inverse_std = lax.rsqrt(jnp.mean(centred * centred, -1, keepdims=True) + 1e-06)
    normed = centred * inverse_std
    scaled = upstream * scales
    return inverse_std * (
        scaled
        - jnp.mean(scaled, -1, keepdims=True)
        - normed * jnp.mean(scaled * normed, -1, keepdims=True)
    )


def on_device(
    llm_grad,
    image_grid,
    image_owner,
    row_start,
    merger_pre,
    vit_out,
    vit_pre,
    ln_gain,
    merger_out_w,
    merger_in_w,
    vit_fc2_w,
):
    seq_count = lax.axis_size(SEQ)
    own_index = lax.axis_index(SEQ)
    grids = image_grid.reshape(seq_count, seq_count, 2)
    counts = grids[:, :, 0] * grids[:, :, 1]
    widths = grids[:, :, 1]
    owners = image_owner.reshape(seq_count, seq_count)
    starts = row_start.reshape(seq_count, seq_count)
    within = jnp.arange(SLOT, dtype=jnp.int32)
    peers = jnp.arange(seq_count, dtype=jnp.int32)
    shard_rows = llm_grad.shape[0]
    my_owners = lax.dynamic_index_in_dim(owners, own_index, 0, keepdims=False)
    my_counts = lax.dynamic_index_in_dim(counts, own_index, 0, keepdims=False)
    my_starts = lax.dynamic_index_in_dim(starts, own_index, 0, keepdims=False)
    targets = (my_owners[None, :] == peers[:, None]).astype(jnp.int32)
    send_counts = jnp.sum(targets * my_counts[None, :], 1)
    send_starts = jnp.sum(targets * my_starts[None, :], 1)
    indices = jnp.minimum(send_starts[:, None] + within[None, :], shard_rows - 1)
    usable = within[None, :] < send_counts[:, None]
    picked = jnp.take(llm_grad, indices.reshape(-1), axis=0)
    outgoing = jnp.where(usable.reshape(-1, 1), picked, jnp.zeros_like(picked)).reshape(
        seq_count, SLOT, llm_grad.shape[1]
    )
    received = (owners == own_index).astype(jnp.int32)
    recv_counts = jnp.sum(received * counts, 1)
    recv_widths = jnp.sum(received * widths, 1)
    wide_rows = lax.all_gather(outgoing, "grp", axis=2, tiled=True)
    flat = wide_rows.reshape(-1, wide_rows.shape[2])
    columns = flat
    folded = jnp.dot(
        columns, gather_axes(merger_out_w, SEQ, (0, 1), 0), preferred_element_type=jnp.float32
    )
    source_grad = folded.astype(jnp.bfloat16).reshape(seq_count, SLOT, merger_out_w.shape[1])
    arrived = lax.all_to_all(source_grad, SEQ, split_axis=0, concat_axis=0, tiled=True)
    unit_grad = arrived.reshape(seq_count * SLOT, merger_out_w.shape[1])
    pre_act = merger_pre[:, 0, :].astype(jnp.float32)
    pre_grad = (gelu_slope(pre_act) * unit_grad.astype(jnp.float32)).astype(jnp.bfloat16)
    merged_part = jnp.dot(
        pre_grad,
        lax.all_gather(merger_in_w, SEQ, axis=1, tiled=True),
        preferred_element_type=jnp.float32,
    )
    vit_width = vit_out.shape[2]
    table = patch_table(recv_widths, recv_counts, SLOT)
    patch_part = jnp.einsum(
        "spq,sqc->spc",
        table,
        merged_part.reshape(seq_count, 4 * SLOT, vit_width),
        precision=lax.Precision.HIGHEST,
    ).reshape(-1, vit_width)
    patch_in = sum_by_parts(patch_part.astype(jnp.bfloat16), "grp").astype(jnp.float32)
    patch_grad = norm_backward(patch_in, vit_out[:, 0, :].astype(jnp.float32), ln_gain).astype(
        jnp.bfloat16
    )
    group_rows = patch_grad.shape[0] // lax.axis_size("grp")
    own_rows = lax.dynamic_slice_in_dim(
        patch_grad, lax.axis_index("grp") * group_rows, group_rows, 0
    )
    columns = patch_grad
    act_grad = jnp.dot(
        columns, gather_directly(vit_fc2_w, SEQ, 0), preferred_element_type=jnp.float32
    )
    fc_in = vit_pre[:, 0, :].astype(jnp.float32)
    sigmoid_q = jax.nn.sigmoid(1.702 * fc_in)
    activation = (fc_in * sigmoid_q).astype(jnp.bfloat16)
    fc1_grad = ((sigmoid_q + 1.702 * fc_in * sigmoid_q * (1.0 - sigmoid_q)) * act_grad).astype(
        jnp.bfloat16
    )
    columns = patch_grad
    weight_grad = sum_at_owner(
        lax.dot_general(
            columns, activation, (((0,), (0,)), ((), ())), preferred_element_type=jnp.float32
        ).astype(jnp.bfloat16),
        SEQ,
        0,
    )
    return (
        own_rows.reshape(group_rows, 1, vit_width),
        fc1_grad.reshape(-1, 1, vit_pre.shape[2]),
        weight_grad,
    )


def solution(mesh):
    finer = Mesh(mesh.devices.reshape(mesh.shape["grp"], 8, 8), ("grp", "seq_0", "seq_1"))
    in_specs = (
        P(SEQ, "grp"),
        P(),
        P(),
        P(),
        P(None, SEQ, "grp"),
        P(None, SEQ, None),
        P(None, SEQ, "grp"),
        P(),
        P(SEQ, "grp"),
        P("grp", SEQ),
        P(SEQ, "grp"),
    )
    out_specs = (P("grp", SEQ, None), P(None, SEQ, "grp"), P(SEQ, "grp"))
    return jax.shard_map(
        on_device, mesh=finer, in_specs=in_specs, out_specs=out_specs, check_vma=False
    )
```

profile of v0, /device:TPU:8, one launch (start us, length us, event | category | flops | bytes accessed | tf_op | source)
XLA Modules:
  0.0 368.1 jit_solution(14716126669979269962)
XLA Ops:
  13.1 30.2 %all-gather = bf16[1024,320]{0,1:T(8,128)(2,1)S(1)} all-gather(bf16[128,320]{0,1:T(8,128)(2,1)S(1)} %copy-done.7), channel_id=2, replica_groups=mesh['grp'=8,'seq_0'=8,'seq_1'=8] {'seq_0'}, dimensions={0}, use_global_device_ids=true | all-gather | bytes 737280 | tf_op jit(solution)/shard_map/all_gather | solution.py:20
  45.1 10.1 %all-gather.7.cloned.1.call-done = bf16[64,3,8192]{2,1,0:T(4,128)(2,1)} async-done(((bf16[64,3,1024]{2,1,0:T(4,128)(2,1)}), bf16[64,3,8192]{2,1,0:T(4,128)(2,1)}) %all-gather.7.cloned.1.call-update) | async-done | bytes 3145744 | tf_op jit(solution)/shard_map/all_gather | solution.py:141
  55.2 7.4 %reshape.530 = bf16[192,8192]{1,0:T(8,128)(2,1)} reshape(bf16[64,3,8192]{2,1,0:T(4,128)(2,1)} %all-gather.7.cloned.1.call-done) | data formatting | bytes 6291456 | tf_op jit(solution)/shard_map/reshape | solution.py:142
  62.6 68.7 %all-gather.9.cloned.1.call-done = bf16[64,128,320]{1,0,2:T(8,128)(2,1)} async-done(((bf16[8,128,320]{1,0,2:T(8,128)(2,1)}), bf16[64,128,320]{1,0,2:T(8,128)(2,1)}) %all-gather.9.cloned.1.call-update) | async-done | bytes 5242896 | tf_op jit(solution)/shard_map/all_gather | solution.py:20
  131.4 4.0 %copy.25 = bf16[8,8,128,320]{2,1,0,3:T(8,128)(2,1)S(1)} copy(bf16[8,8,128,320]{2,0,1,3:T(8,128)(2,1)} %bitcast.87) | data formatting | bytes 10485760 | tf_op jit(solution)/shard_map/transpose | solution.py:24
  135.4 4.3 %fusion.9 = bf16[192,320]{1,0:T(8,128)(2,1)S(1)} fusion(bf16[192,8192]{1,0:T(8,128)(2,1)S(1)} %copy-done.4, bf16[40,8,64,128]{3,2,1,0:T(8,128)(2,1)S(1)} %bitcast.88), kind=kOutput, calls=%fused_computation.23 | convolution fusion | flops 1006694400 | bytes 8511488 | tf_op jit(solution)/shard_map/dot_general | solution.py:144
  140.5 10.7 %all-to-all-start = ((bf16[64,3,320]{2,1,0:T(4,128)(2,1)}), bf16[64,3,320]{2,1,0:T(4,128)(2,1)S(1)}, u32[]{:S(2)}, u32[]{:S(2)}) async-start(bf16[64,3,320]{2,1,0:T(4,128)(2,1)} %reshape.532), calls=%async_computation | async-start | bytes 393216 | tf_op jit(solution)/shard_map/all_to_all | solution.py:148
  152.0 11.8 %all-to-all-done = bf16[64,3,320]{2,1,0:T(4,128)(2,1)S(1)} async-done(((bf16[64,3,320]{2,1,0:T(4,128)(2,1)}), bf16[64,3,320]{2,1,0:T(4,128)(2,1)S(1)}, u32[]{:S(2)}, u32[]{:S(2)}) %all-to-all-start) | async-done | bytes 122912 | tf_op jit(solution)/shard_map/all_to_all | solution.py:148
  163.9 56.5 %all-gather.11.cloned.1.call-done = bf16[320,5120]{0,1:T(8,128)(2,1)} async-done(((bf16[320,80]{0,1:T(8,128)(2,1)}), bf16[320,5120]{0,1:T(8,128)(2,1)}) %all-gather.11.cloned.1.call-update) | async-done | bytes 3276816 | tf_op jit(solution)/shard_map/all_gather | solution.py:154
  220.4 5.6 %fusion.43 = f32[192,5120]{1,0:T(8,128)} fusion(bf16[320,5120]{0,1:T(8,128)(2,1)} %all-gather.11.cloned.1.call-done, f32[192,320]{1,0:T(8,128)S(1)} %reshape.539, bf16[192,1,320]{2,0,1:T(8,128)(2,1)S(1)} %copy-done.6), kind=kOutput, calls=%fused_computation.61 | convolution fusion | flops 629821440 | bytes 7577600 | tf_op jit(solution)/shard_map/dot_general | solution.py:152
  226.0 5.4 %reshape.533 = f32[64,12,1280]{2,1,0:T(8,128)} reshape(f32[192,5120]{1,0:T(8,128)} %fusion.43) | data formatting | bytes 7864320 | tf_op jit(solution)/shard_map/reshape | solution.py:162
  231.3 5.3 %convolution_convert_fusion = bf16[64,12,1280]{2,1,0:T(8,128)(2,1)S(1)} fusion(f32[64,12,1280]{2,1,0:T(8,128)} %reshape.533, s32[64,12]{1,0:T(8,128)S(1)} %copy.20, pred[64,12]{1,0:T(8,128)(4,1)S(1)} %copy.21), kind=kOutput, calls=%fused_computation.9 | convolution fusion | flops 142559232 | bytes 5902080 | tf_op jit(solution)/shard_map/spq,sqc->spc/dot_general | solution.py:159
  236.6 2.0 convert_element_type.91
  238.7 35.5 %reduce-scatter.2.cloned.1.call-done = bf16[96,1280]{1,0:T(8,128)(2,1)} async-done(((bf16[768,1280]{1,0:T(8,128)(2,1)}), bf16[96,1280]{1,0:T(8,128)(2,1)}) %reduce-scatter.2.cloned.1.call-update) | async-done | bytes 245776 | tf_op jit(solution)/shard_map/reduce_scatter | solution.py:40
  275.3 13.5 %all-to-all-start.1 = ((bf16[64,20,320]{2,1,0:T(8,128)(2,1)}), bf16[64,20,320]{2,1,0:T(8,128)(2,1)}, u32[]{:S(2)}, u32[]{:S(2)}) async-start(bf16[64,20,320]{2,1,0:T(8,128)(2,1)} %broadcast_in_dim.34), calls=%async_computation.2 | async-start | bytes 2359296 | tf_op jit(solution)/shard_map/all_to_all | solution.py:49
  289.3 2.4 multiply_reduce_fusion.1
  291.8 13.8 %all-gather.13.cloned.1.call-done = bf16[768,1280]{1,0:T(8,128)(2,1)} async-done(((bf16[96,1280]{1,0:T(8,128)(2,1)}), bf16[768,1280]{1,0:T(8,128)(2,1)}) %all-gather.13.cloned.1.call-update) | async-done | bytes 1966096 | tf_op jit(solution)/shard_map/all_gather | solution.py:43
  305.6 1.8 convert_element_type.111
  314.7 3.8 %all-to-all-done.1 = bf16[64,20,320]{2,1,0:T(8,128)(2,1)} async-done(((bf16[64,20,320]{2,1,0:T(8,128)(2,1)}), bf16[64,20,320]{2,1,0:T(8,128)(2,1)}, u32[]{:S(2)}, u32[]{:S(2)}) %all-to-all-start.1) | async-done | bytes 819232 | tf_op jit(solution)/shard_map/all_to_all | solution.py:49
  318.5 9.6 %all-to-all-start.2 = ((bf16[64,20,320]{2,1,0:T(8,128)(2,1)}), bf16[64,20,320]{2,1,0:T(8,128)(2,1)S(1)}, u32[]{:S(2)}, u32[]{:S(2)}) async-start(bf16[64,20,320]{2,1,0:T(8,128)(2,1)} %reshape.537), calls=%async_computation.3 | async-start | bytes 2359296 | tf_op jit(solution)/shard_map/all_to_all | solution.py:64
  328.2 1.5 reshape.535
  330.0 3.5 fusion.4
  333.4 2.0 fusion.42
  335.4 25.2 %all-to-all-done.2 = bf16[64,20,320]{2,1,0:T(8,128)(2,1)S(1)} async-done(((bf16[64,20,320]{2,1,0:T(8,128)(2,1)}), bf16[64,20,320]{2,1,0:T(8,128)(2,1)S(1)}, u32[]{:S(2)}, u32[]{:S(2)}) %all-to-all-start.2) | async-done | bytes 819232 | tf_op jit(solution)/shard_map/all_to_all | solution.py:64
  (80 shorter events, 19.3 us)
Async XLA Ops:
  7.2 3.1 copy-start
  7.2 5.9 %copy-start.7 = (bf16[128,320]{0,1:T(8,128)(2,1)S(1)}, bf16[128,320]{0,1:T(8,128)(2,1)}, u32[]{:S(2)}) copy-start(bf16[128,320]{0,1:T(8,128)(2,1)} %param.19) | copy-start | bytes 245764
  7.2 48.0 %all-gather.7.cloned.1.call-start = ((), (), s32[]{:S(2)}) async-start(), calls=%async_computation.4 | async-start | bytes 4718592 | tf_op jit(solution)/shard_map/all_gather | solution.py:141
  13.0 118.3 %all-gather.9.cloned.1.call-start = ((), (), s32[]{:S(2)}) async-start(), calls=%async_computation.5 | async-start | bytes 5898240 | tf_op jit(solution)/shard_map/all_gather | solution.py:20
  44.3 176.1 %all-gather.11.cloned.1.call-start = ((), (), s32[]{:S(2)}) async-start(), calls=%async_computation.6 | async-start | bytes 3993600 | tf_op jit(solution)/shard_map/all_gather | solution.py:154
  131.4 4.0 %copy-start.4 = (bf16[192,8192]{1,0:T(8,128)(2,1)S(1)}, bf16[192,8192]{1,0:T(8,128)(2,1)}, u32[]{:S(2)}) copy-start(bf16[192,8192]{1,0:T(8,128)(2,1)} %reshape.530) | copy-start | bytes 9437188
  135.4 85.0 %copy-start.6 = (bf16[192,1,320]{2,0,1:T(8,128)(2,1)S(1)}, bf16[192,1,320]{2,0,1:T(8,128)(2,1)}, u32[]{:S(2)}) copy-start(bf16[192,1,320]{2,0,1:T(8,128)(2,1)} %param.15) | copy-start | bytes 368644
  140.5 23.3 %all-to-all-start = ((bf16[64,3,320]{2,1,0:T(4,128)(2,1)}), bf16[64,3,320]{2,1,0:T(4,128)(2,1)S(1)}, u32[]{:S(2)}, u32[]{:S(2)}) async-start(bf16[64,3,320]{2,1,0:T(4,128)(2,1)} %reshape.532), calls=%async_computation | async-start | bytes 393216 | tf_op jit(solution)/shard_map/all_to_all | solution.py:148
  151.2 123.0 %reduce-scatter.2.cloned.1.call-start = ((), (), s32[]{:S(2)}) async-start(), calls=%async_computation.7 | async-start | bytes 2211840 | tf_op jit(solution)/shard_map/reduce_scatter | solution.py:40
  236.6 37.6 %copy-start.9 = (bf16[20,320]{1,0:T(8,128)(2,1)S(1)}, bf16[20,320]{1,0:T(8,128)(2,1)}, u32[]{:S(2)}) copy-start(bf16[20,320]{1,0:T(8,128)(2,1)} %param.21) | copy-start | bytes 38404
  238.7 50.2 %copy-start.3 = (bf16[768,1,1280]{2,0,1:T(8,128)(2,1)S(1)}, bf16[768,1,1280]{2,0,1:T(8,128)(2,1)}, u32[]{:S(2)}) copy-start(bf16[768,1,1280]{2,0,1:T(8,128)(2,1)} %param.16) | copy-start | bytes 5898244
  238.7 66.9 %all-gather.13.cloned.1.call-start = ((), (), s32[]{:S(2)}) async-start(), calls=%async_computation.8 | async-start | bytes 2211840 | tf_op jit(solution)/shard_map/all_gather | solution.py:43
  275.3 43.2 %all-to-all-start.1 = ((bf16[64,20,320]{2,1,0:T(8,128)(2,1)}), bf16[64,20,320]{2,1,0:T(8,128)(2,1)}, u32[]{:S(2)}, u32[]{:S(2)}) async-start(bf16[64,20,320]{2,1,0:T(8,128)(2,1)} %broadcast_in_dim.34), calls=%async_computation.2 | async-start | bytes 2359296 | tf_op jit(solution)/shard_map/all_to_all | solution.py:49
  291.7 15.7 %copy-start.8 = (f32[1280]{0:T(1024)S(1)}, f32[1280]{0:T(1024)}, u32[]{:S(2)}) copy-start(f32[1280]{0:T(1024)} %param.18) | copy-start | bytes 15364
  307.4 1.9 copy-start.2
  309.3 2.6 copy-start.10
  310.5 1.4 copy-start.5
  318.5 42.2 %all-to-all-start.2 = ((bf16[64,20,320]{2,1,0:T(8,128)(2,1)}), bf16[64,20,320]{2,1,0:T(8,128)(2,1)S(1)}, u32[]{:S(2)}, u32[]{:S(2)}) async-start(bf16[64,20,320]{2,1,0:T(8,128)(2,1)} %reshape.537), calls=%async_computation.3 | async-start | bytes 2359296 | tf_op jit(solution)/shard_map/all_to_all | solution.py:64
  329.9 31.7 %copy-start.1 = (bf16[256,1024]{1,0:T(8,128)(2,1)S(1)}, bf16[256,1024]{1,0:T(8,128)(2,1)}, u32[]{:S(2)}) copy-start(bf16[256,1024]{1,0:T(8,128)(2,1)} %param.11) | copy-start | bytes 1572868
Sparse Core Ops, SparseCore 0:
  13.2 41.9 all-gather.6
  57.2 74.1 all-gather.8
  134.4 85.9 all-gather.10
  238.8 35.3 reduce-scatter.1
  276.4 29.1 all-gather.12
where the time goes:
time: 369 us; the launch traced here: 368 us
  waiting for transfers between devices  226 us (61%)
  starting transfers between devices  34.1 us (9%)
  local copies, waits for them, and re-layouts  32 us (9%)
  blocking collectives  30.2 us (8%)
  matrix products  19.6 us (5%)
  between operations  14.1 us (4%)
  other arithmetic  11.9 us (3%)
    all_gather x1, waiting for transfers between devices, gather_in_order(): tiles = lax.all_gather(tiles, axes[k], axis=0, tiled=True)  68.7 us
    all_gather x1, waiting for transfers between devices, on_device(): lax.all_gather(merger_in_w, SEQ, axis=1, tiled=True)  56.5 us
    reduce_scatter x1, waiting for transfers between devices, sum_by_parts(): lax.psum_scatter(filled_up(lines, lax.axis_size(axis)), axis, scatter_dim...  35.5 us
    all_gather x1, blocking collectives, gather_in_order(): tiles = lax.all_gather(tiles, axes[k], axis=0, tiled=True)  30.2 us
    all_to_all x1, waiting for transfers between devices, sum_at_owner(): lax.all_to_all(tiles, axis, split_axis=0, concat_axis=0, tiled=True)  25.2 us
    all_gather x1, waiting for transfers between devices, sum_by_parts(): whole = lax.all_gather(own, axis).reshape(-1, *lines.shape[1:])  13.8 us
    all_to_all x1, starting transfers between devices, copy_for_each(): return lax.all_to_all(copies, axis, split_axis=0, concat_axis=0, tiled=True)  13.5 us
    all_to_all x1, waiting for transfers between devices, on_device(): lax.all_to_all(source_grad, SEQ, split_axis=0, concat_axis=0, tiled=True)  11.8 us
  transfers between devices with their start and end apart: 8, of which 8 were waited for; matrix products, arithmetic and copies ran while one was open for 10% of the time, Pallas kernels for 0%

commit v1 on v0

--- a/solution.py
+++ b/solution.py
@@ -138,7 +138,12 @@
     received = (owners == own_index).astype(jnp.int32)
     recv_counts = jnp.sum(received * counts, 1)
     recv_widths = jnp.sum(received * widths, 1)
-    wide_rows = lax.all_gather(outgoing, "grp", axis=2, tiled=True)
+    ring = [outgoing]
+    for hop in range(7):
+        ring.append(lax.ppermute(ring[-1], "grp", [(dev, (dev + 1) % 8) for dev in range(8)]))
+    wide_rows = jnp.roll(
+        jnp.concatenate(ring[::-1], axis=2), (lax.axis_index("grp") + 1) * ring[0].shape[2], axis=2
+    )
     flat = wide_rows.reshape(-1, wide_rows.shape[2])
     columns = flat
     folded = jnp.dot(

time: 369 us -> 351 us (0.951)
  waiting for transfers between devices: 226 us -> 198 us
  local copies, waits for them, and re-layouts: 32 us -> 41.2 us
    ppermute x0 -> x7, waiting for transfers between devices: none -> 68.9 us  [on_device(): lax.ppermute(ring[-1], 'grp', [(dev, (dev + 1) % 8) for dev in range(8)])]
    all_gather x1, waiting for transfers between devices: 68.7 us -> 0.01 us  [gather_in_order(): tiles = lax.all_gather(tiles, axes[k], axis=0, tiled=True)]
    all_gather x1, waiting for transfers between devices: 56.5 us -> 38.2 us  [on_device(): lax.all_gather(merger_in_w, SEQ, axis=1, tiled=True)]
    all_gather x1 -> x0, waiting for transfers between devices: 10.1 us -> none  [on_device(): wide_rows = lax.all_gather(outgoing, 'grp', axis=2, tiled=True)]
    unnamed x23 -> x35, local copies, waits for them, and re-layouts: 2.94 us -> 8.38 us
    dynamic_slice x0 -> x1, local copies, waits for them, and re-layouts: none -> 3.84 us  [on_device(): jnp.roll(jnp.concatenate(ring[::-1], axis=2), (lax.axis_index('grp') + 1)...]
  transfers between devices with their start and end apart: 8 -> 14, of which waited for: 8 -> 13; matrix products, arithmetic and copies ran while one was open for 10% -> 15% of each run, Pallas kernels for 0% -> 0%
where the time goes in v1:
time: 351 us; the launch traced here: 350 us
  waiting for transfers between devices  198 us (56%)
  local copies, waits for them, and re-layouts  41.2 us (12%)
  starting transfers between devices  34.6 us (10%)
  blocking collectives  30.6 us (9%)
  matrix products  19.6 us (6%)
  between operations  14.2 us (4%)
  other arithmetic  12.2 us (3%)
    ppermute x7, waiting for transfers between devices, on_device(): lax.ppermute(ring[-1], 'grp', [(dev, (dev + 1) % 8) for dev in range(8)])  68.9 us
    all_gather x1, waiting for transfers between devices, on_device(): lax.all_gather(merger_in_w, SEQ, axis=1, tiled=True)  38.2 us
    reduce_scatter x1, waiting for transfers between devices, sum_by_parts(): lax.psum_scatter(filled_up(lines, lax.axis_size(axis)), axis, scatter_dim...  35.4 us
    all_gather x1, blocking collectives, gather_in_order(): tiles = lax.all_gather(tiles, axes[k], axis=0, tiled=True)  30.6 us
    all_to_all x1, waiting for transfers between devices, sum_at_owner(): lax.all_to_all(tiles, axis, split_axis=0, concat_axis=0, tiled=True)  25.2 us
    all_gather x1, waiting for transfers between devices, sum_by_parts(): whole = lax.all_gather(own, axis).reshape(-1, *lines.shape[1:])  13.8 us
    all_to_all x1, starting transfers between devices, copy_for_each(): return lax.all_to_all(copies, axis, split_axis=0, concat_axis=0, tiled=True)  13.5 us
    all_to_all x1, waiting for transfers between devices, on_device(): lax.all_to_all(source_grad, SEQ, split_axis=0, concat_axis=0, tiled=True)  12.1 us
  transfers between devices with their start and end apart: 14, of which 13 were waited for; matrix products, arithmetic and copies ran while one was open for 15% of the time, Pallas kernels for 0%

profile of v1, /device:TPU:8, one launch (start us, length us, event | category | flops | bytes accessed | tf_op | source)
XLA Modules:
  0.0 349.8 jit_solution(13209908474489686308)
XLA Ops:
  7.2 30.6 %all-gather = bf16[1024,320]{0,1:T(8,128)(2,1)S(1)} all-gather(bf16[128,320]{0,1:T(8,128)(2,1)} %param.19), channel_id=2, replica_groups=mesh['grp'=8,'seq_0'=8,'seq_1'=8] {'seq_0'}, dimensions={0}, use_global_device_ids=true | all-gather | bytes 737280 | tf_op jit(solution)/shard_map/all_gather | solution.py:20
  43.8 9.8 %collective-permute-done = bf16[64,3,1024]{2,1,0:T(4,128)(2,1)S(1)} collective-permute-done((bf16[64,3,1024]{2,1,0:T(4,128)(2,1)S(1)}, bf16[64,3,1024]{2,1,0:T(4,128)(2,1)S(1)}, u32[]{:S(2)}, u32[]{:S(2)}) %collective-permute-start) | collective-permute-done | bytes 393248 | tf_op jit(solution)/shard_map/ppermute | solution.py:143
  53.6 9.8 %collective-permute-done.1 = bf16[64,3,1024]{2,1,0:T(4,128)(2,1)S(1)} collective-permute-done((bf16[64,3,1024]{2,1,0:T(4,128)(2,1)S(1)}, bf16[64,3,1024]{2,1,0:T(4,128)(2,1)S(1)}, u32[]{:S(2)}, u32[]{:S(2)}) %collective-permute-start.1) | collective-permute-done | bytes 393248 | tf_op jit(solution)/shard_map/ppermute | solution.py:143
  63.4 9.8 %collective-permute-done.2 = bf16[64,3,1024]{2,1,0:T(4,128)(2,1)S(1)} collective-permute-done((bf16[64,3,1024]{2,1,0:T(4,128)(2,1)S(1)}, bf16[64,3,1024]{2,1,0:T(4,128)(2,1)S(1)}, u32[]{:S(2)}, u32[]{:S(2)}) %collective-permute-start.2) | collective-permute-done | bytes 393248 | tf_op jit(solution)/shard_map/ppermute | solution.py:143
  73.3 9.8 %collective-permute-done.3 = bf16[64,3,1024]{2,1,0:T(4,128)(2,1)S(1)} collective-permute-done((bf16[64,3,1024]{2,1,0:T(4,128)(2,1)S(1)}, bf16[64,3,1024]{2,1,0:T(4,128)(2,1)S(1)}, u32[]{:S(2)}, u32[]{:S(2)}) %collective-permute-start.3) | collective-permute-done | bytes 393248 | tf_op jit(solution)/shard_map/ppermute | solution.py:143
  83.1 9.8 %collective-permute-done.4 = bf16[64,3,1024]{2,1,0:T(4,128)(2,1)S(1)} collective-permute-done((bf16[64,3,1024]{2,1,0:T(4,128)(2,1)S(1)}, bf16[64,3,1024]{2,1,0:T(4,128)(2,1)S(1)}, u32[]{:S(2)}, u32[]{:S(2)}) %collective-permute-start.4) | collective-permute-done | bytes 393248 | tf_op jit(solution)/shard_map/ppermute | solution.py:143
  92.9 9.9 %collective-permute-done.5 = bf16[64,3,1024]{2,1,0:T(4,128)(2,1)} collective-permute-done((bf16[64,3,1024]{2,1,0:T(4,128)(2,1)S(1)}, bf16[64,3,1024]{2,1,0:T(4,128)(2,1)}, u32[]{:S(2)}, u32[]{:S(2)}) %collective-permute-start.5) | collective-permute-done | bytes 393248 | tf_op jit(solution)/shard_map/ppermute | solution.py:143
  102.8 10.0 %collective-permute-done.6 = bf16[64,3,1024]{2,1,0:T(4,128)(2,1)S(1)} collective-permute-done((bf16[64,3,1024]{2,1,0:T(4,128)(2,1)}, bf16[64,3,1024]{2,1,0:T(4,128)(2,1)S(1)}, u32[]{:S(2)}, u32[]{:S(2)}) %collective-permute-start.6) | collective-permute-done | bytes 393248 | tf_op jit(solution)/shard_map/ppermute | solution.py:143
  119.5 3.8 %constant_dynamic-slice_fusion = bf16[64,3,8192]{2,1,0:T(4,128)(2,1)} fusion(bf16[64,3,16384]{2,1,0:T(4,128)(2,1)S(1)} %constant_dynamic-update-slice_fusion, s32[]{:T(128)S(6)} %select_n.148), kind=kLoop, calls=%fused_computation.124 | loop fusion | bytes 6291460 | tf_op jit(solution)/shard_map/jit(_roll_dynamic)/dynamic_slice | solution.py:144
  123.3 7.4 %reshape.530 = bf16[192,8192]{1,0:T(8,128)(2,1)} reshape(bf16[64,3,8192]{2,1,0:T(4,128)(2,1)} %constant_dynamic-slice_fusion) | data formatting | bytes 6291456 | tf_op jit(solution)/shard_map/reshape | solution.py:147
  130.7 4.0 %copy.25 = bf16[8,8,128,320]{2,1,0,3:T(8,128)(2,1)S(1)} copy(bf16[8,8,128,320]{2,0,1,3:T(8,128)(2,1)} %bitcast.87) | data formatting | bytes 10485760 | tf_op jit(solution)/shard_map/transpose | solution.py:24
  134.8 4.3 %fusion.9 = bf16[192,320]{1,0:T(8,128)(2,1)S(1)} fusion(bf16[192,8192]{1,0:T(8,128)(2,1)S(1)} %copy-done.4, bf16[40,8,64,128]{3,2,1,0:T(8,128)(2,1)S(1)} %bitcast.88), kind=kOutput, calls=%fused_computation.23 | convolution fusion | flops 1006694400 | bytes 8511488 | tf_op jit(solution)/shard_map/dot_general | solution.py:149
  139.9 11.3 %all-to-all-start = ((bf16[64,3,320]{2,1,0:T(4,128)(2,1)}), bf16[64,3,320]{2,1,0:T(4,128)(2,1)S(1)}, u32[]{:S(2)}, u32[]{:S(2)}) async-start(bf16[64,3,320]{2,1,0:T(4,128)(2,1)} %reshape.532), calls=%async_computation | async-start | bytes 393216 | tf_op jit(solution)/shard_map/all_to_all | solution.py:153
  151.8 12.1 %all-to-all-done = bf16[64,3,320]{2,1,0:T(4,128)(2,1)S(1)} async-done(((bf16[64,3,320]{2,1,0:T(4,128)(2,1)}), bf16[64,3,320]{2,1,0:T(4,128)(2,1)S(1)}, u32[]{:S(2)}, u32[]{:S(2)}) %all-to-all-start) | async-done | bytes 122912 | tf_op jit(solution)/shard_map/all_to_all | solution.py:153
  164.0 38.2 %all-gather.8.cloned.1.call-done = bf16[320,5120]{0,1:T(8,128)(2,1)} async-done(((bf16[320,80]{0,1:T(8,128)(2,1)}), bf16[320,5120]{0,1:T(8,128)(2,1)}) %all-gather.8.cloned.1.call-update) | async-done | bytes 3276816 | tf_op jit(solution)/shard_map/all_gather | solution.py:159
  202.2 5.6 %fusion.43 = f32[192,5120]{1,0:T(8,128)} fusion(bf16[320,5120]{0,1:T(8,128)(2,1)} %all-gather.8.cloned.1.call-done, f32[192,320]{1,0:T(8,128)S(1)} %reshape.539, bf16[192,1,320]{2,0,1:T(8,128)(2,1)S(1)} %copy-done.6), kind=kOutput, calls=%fused_computation.61 | convolution fusion | flops 629821440 | bytes 7577600 | tf_op jit(solution)/shard_map/dot_general | solution.py:157
  207.7 5.4 %reshape.533 = f32[64,12,1280]{2,1,0:T(8,128)} reshape(f32[192,5120]{1,0:T(8,128)} %fusion.43) | data formatting | bytes 7864320 | tf_op jit(solution)/shard_map/reshape | solution.py:167
  213.1 5.3 %convolution_convert_fusion = bf16[64,12,1280]{2,1,0:T(8,128)(2,1)S(1)} fusion(f32[64,12,1280]{2,1,0:T(8,128)} %reshape.533, s32[64,12]{1,0:T(8,128)S(1)} %copy.20, pred[64,12]{1,0:T(8,128)(4,1)S(1)} %copy.21), kind=kOutput, calls=%fused_computation.9 | convolution fusion | flops 142559232 | bytes 5902080 | tf_op jit(solution)/shard_map/spq,sqc->spc/dot_general | solution.py:164
  220.5 35.4 %reduce-scatter.2.cloned.1.call-done = bf16[96,1280]{1,0:T(8,128)(2,1)} async-done(((bf16[768,1280]{1,0:T(8,128)(2,1)}), bf16[96,1280]{1,0:T(8,128)(2,1)}) %reduce-scatter.2.cloned.1.call-update) | async-done | bytes 245776 | tf_op jit(solution)/shard_map/reduce_scatter | solution.py:40
  257.0 13.5 %all-to-all-start.1 = ((bf16[64,20,320]{2,1,0:T(8,128)(2,1)}), bf16[64,20,320]{2,1,0:T(8,128)(2,1)}, u32[]{:S(2)}, u32[]{:S(2)}) async-start(bf16[64,20,320]{2,1,0:T(8,128)(2,1)} %broadcast_in_dim.34), calls=%async_computation.2 | async-start | bytes 2359296 | tf_op jit(solution)/shard_map/all_to_all | solution.py:49
  273.5 13.8 %all-gather.10.cloned.1.call-done = bf16[768,1280]{1,0:T(8,128)(2,1)} async-done(((bf16[96,1280]{1,0:T(8,128)(2,1)}), bf16[768,1280]{1,0:T(8,128)(2,1)}) %all-gather.10.cloned.1.call-update) | async-done | bytes 1966096 | tf_op jit(solution)/shard_map/all_gather | solution.py:43
  296.4 3.8 %all-to-all-done.1 = bf16[64,20,320]{2,1,0:T(8,128)(2,1)} async-done(((bf16[64,20,320]{2,1,0:T(8,128)(2,1)}), bf16[64,20,320]{2,1,0:T(8,128)(2,1)}, u32[]{:S(2)}, u32[]{:S(2)}) %all-to-all-start.1) | async-done | bytes 819232 | tf_op jit(solution)/shard_map/all_to_all | solution.py:49
  300.2 9.5 %all-to-all-start.2 = ((bf16[64,20,320]{2,1,0:T(8,128)(2,1)}), bf16[64,20,320]{2,1,0:T(8,128)(2,1)S(1)}, u32[]{:S(2)}, u32[]{:S(2)}) async-start(bf16[64,20,320]{2,1,0:T(8,128)(2,1)} %reshape.537), calls=%async_computation.3 | async-start | bytes 2359296 | tf_op jit(solution)/shard_map/all_to_all | solution.py:64
  317.2 25.2 %all-to-all-done.2 = bf16[64,20,320]{2,1,0:T(8,128)(2,1)S(1)} async-done(((bf16[64,20,320]{2,1,0:T(8,128)(2,1)}), bf16[64,20,320]{2,1,0:T(8,128)(2,1)S(1)}, u32[]{:S(2)}, u32[]{:S(2)}) %all-to-all-start.2) | async-done | bytes 819232 | tf_op jit(solution)/shard_map/all_to_all | solution.py:64
  (106 shorter events, 37.4 us)
Async XLA Ops:
  7.2 34.7 %copy-start = (bf16[256,1024]{1,0:T(8,128)(2,1)S(1)}, bf16[256,1024]{1,0:T(8,128)(2,1)}, u32[]{:S(2)}) copy-start(bf16[256,1024]{1,0:T(8,128)(2,1)} %param.11) | copy-start | bytes 1572868
  7.2 123.6 %all-gather.6.cloned.1.call-start = ((), (), s32[]{:S(2)}) async-start(), calls=%async_computation.4 | async-start | bytes 5898240 | tf_op jit(solution)/shard_map/all_gather | solution.py:20
  38.8 163.3 %all-gather.8.cloned.1.call-start = ((), (), s32[]{:S(2)}) async-start(), calls=%async_computation.5 | async-start | bytes 3993600 | tf_op jit(solution)/shard_map/all_gather | solution.py:159
  43.8 9.8 %collective-permute-start = (bf16[64,3,1024]{2,1,0:T(4,128)(2,1)S(1)}, bf16[64,3,1024]{2,1,0:T(4,128)(2,1)S(1)}, u32[]{:S(2)}, u32[]{:S(2)}) collective-permute-start(bf16[64,3,1024]{2,1,0:T(4,128)(2,1)S(1)} %select_select_fusion), channel_id=1, source_target_pairs={{0,64},{64,128},{128,192},{192,256},{256,320},{320,384},{384,448},... | collective-permute-start | bytes 1179656 | tf_op jit(solution)/shard_map/ppermute | solution.py:143
  53.6 9.8 %collective-permute-start.1 = (bf16[64,3,1024]{2,1,0:T(4,128)(2,1)S(1)}, bf16[64,3,1024]{2,1,0:T(4,128)(2,1)S(1)}, u32[]{:S(2)}, u32[]{:S(2)}) collective-permute-start(bf16[64,3,1024]{2,1,0:T(4,128)(2,1)S(1)} %collective-permute-done), channel_id=1, source_target_pairs={{0,64},{64,128},{128,192},{192,256},{256,320},{320,384},{384,448},... | collective-permute-start | bytes 1179656 | tf_op jit(solution)/shard_map/ppermute | solution.py:143
  63.4 9.8 %collective-permute-start.2 = (bf16[64,3,1024]{2,1,0:T(4,128)(2,1)S(1)}, bf16[64,3,1024]{2,1,0:T(4,128)(2,1)S(1)}, u32[]{:S(2)}, u32[]{:S(2)}) collective-permute-start(bf16[64,3,1024]{2,1,0:T(4,128)(2,1)S(1)} %collective-permute-done.1), channel_id=1, source_target_pairs={{0,64},{64,128},{128,192},{192,256},{256,320},{320,384},{384,448},... | collective-permute-start | bytes 1179656 | tf_op jit(solution)/shard_map/ppermute | solution.py:143
  73.2 9.8 %collective-permute-start.3 = (bf16[64,3,1024]{2,1,0:T(4,128)(2,1)S(1)}, bf16[64,3,1024]{2,1,0:T(4,128)(2,1)S(1)}, u32[]{:S(2)}, u32[]{:S(2)}) collective-permute-start(bf16[64,3,1024]{2,1,0:T(4,128)(2,1)S(1)} %collective-permute-done.2), channel_id=1, source_target_pairs={{0,64},{64,128},{128,192},{192,256},{256,320},{320,384},{384,448},... | collective-permute-start | bytes 1179656 | tf_op jit(solution)/shard_map/ppermute | solution.py:143
  83.1 9.8 %collective-permute-start.4 = (bf16[64,3,1024]{2,1,0:T(4,128)(2,1)S(1)}, bf16[64,3,1024]{2,1,0:T(4,128)(2,1)S(1)}, u32[]{:S(2)}, u32[]{:S(2)}) collective-permute-start(bf16[64,3,1024]{2,1,0:T(4,128)(2,1)S(1)} %collective-permute-done.3), channel_id=1, source_target_pairs={{0,64},{64,128},{128,192},{192,256},{256,320},{320,384},{384,448},... | collective-permute-start | bytes 1179656 | tf_op jit(solution)/shard_map/ppermute | solution.py:143
  92.9 9.9 %collective-permute-start.5 = (bf16[64,3,1024]{2,1,0:T(4,128)(2,1)S(1)}, bf16[64,3,1024]{2,1,0:T(4,128)(2,1)}, u32[]{:S(2)}, u32[]{:S(2)}) collective-permute-start(bf16[64,3,1024]{2,1,0:T(4,128)(2,1)S(1)} %collective-permute-done.4), channel_id=1, source_target_pairs={{0,64},{64,128},{128,192},{192,256},{256,320},{320,384},{384,448},... | collective-permute-start | bytes 1179656 | tf_op jit(solution)/shard_map/ppermute | solution.py:143
  102.8 10.0 %collective-permute-start.6 = (bf16[64,3,1024]{2,1,0:T(4,128)(2,1)}, bf16[64,3,1024]{2,1,0:T(4,128)(2,1)S(1)}, u32[]{:S(2)}, u32[]{:S(2)}) collective-permute-start(bf16[64,3,1024]{2,1,0:T(4,128)(2,1)} %collective-permute-done.5), channel_id=1, source_target_pairs={{0,64},{64,128},{128,192},{192,256},{256,320},{320,384},{384,448},... | collective-permute-start | bytes 1179656 | tf_op jit(solution)/shard_map/ppermute | solution.py:143
  130.7 4.0 %copy-start.4 = (bf16[192,8192]{1,0:T(8,128)(2,1)S(1)}, bf16[192,8192]{1,0:T(8,128)(2,1)}, u32[]{:S(2)}) copy-start(bf16[192,8192]{1,0:T(8,128)(2,1)} %reshape.530) | copy-start | bytes 9437188
  134.8 67.4 %copy-start.6 = (bf16[192,1,320]{2,0,1:T(8,128)(2,1)S(1)}, bf16[192,1,320]{2,0,1:T(8,128)(2,1)}, u32[]{:S(2)}) copy-start(bf16[192,1,320]{2,0,1:T(8,128)(2,1)} %param.15) | copy-start | bytes 368644
  139.9 24.0 %all-to-all-start = ((bf16[64,3,320]{2,1,0:T(4,128)(2,1)}), bf16[64,3,320]{2,1,0:T(4,128)(2,1)S(1)}, u32[]{:S(2)}, u32[]{:S(2)}) async-start(bf16[64,3,320]{2,1,0:T(4,128)(2,1)} %reshape.532), calls=%async_computation | async-start | bytes 393216 | tf_op jit(solution)/shard_map/all_to_all | solution.py:153
  151.2 104.7 %reduce-scatter.2.cloned.1.call-start = ((), (), s32[]{:S(2)}) async-start(), calls=%async_computation.6 | async-start | bytes 2211840 | tf_op jit(solution)/shard_map/reduce_scatter | solution.py:40
  218.4 37.6 %copy-start.8 = (bf16[20,320]{1,0:T(8,128)(2,1)S(1)}, bf16[20,320]{1,0:T(8,128)(2,1)}, u32[]{:S(2)}) copy-start(bf16[20,320]{1,0:T(8,128)(2,1)} %param.21) | copy-start | bytes 38404
  220.4 50.2 %copy-start.3 = (bf16[768,1,1280]{2,0,1:T(8,128)(2,1)S(1)}, bf16[768,1,1280]{2,0,1:T(8,128)(2,1)}, u32[]{:S(2)}) copy-start(bf16[768,1,1280]{2,0,1:T(8,128)(2,1)} %param.16) | copy-start | bytes 5898244
  220.4 66.9 %all-gather.10.cloned.1.call-start = ((), (), s32[]{:S(2)}) async-start(), calls=%async_computation.7 | async-start | bytes 2211840 | tf_op jit(solution)/shard_map/all_gather | solution.py:43
  257.0 43.2 %all-to-all-start.1 = ((bf16[64,20,320]{2,1,0:T(8,128)(2,1)}), bf16[64,20,320]{2,1,0:T(8,128)(2,1)}, u32[]{:S(2)}, u32[]{:S(2)}) async-start(bf16[64,20,320]{2,1,0:T(8,128)(2,1)} %broadcast_in_dim.34), calls=%async_computation.2 | async-start | bytes 2359296 | tf_op jit(solution)/shard_map/all_to_all | solution.py:49
  273.4 15.7 %copy-start.7 = (f32[1280]{0:T(1024)S(1)}, f32[1280]{0:T(1024)}, u32[]{:S(2)}) copy-start(f32[1280]{0:T(1024)} %param.18) | copy-start | bytes 15364
  289.1 1.9 copy-start.2
  291.0 2.5 copy-start.9
  292.2 1.4 copy-start.5
  300.2 42.2 %all-to-all-start.2 = ((bf16[64,20,320]{2,1,0:T(8,128)(2,1)}), bf16[64,20,320]{2,1,0:T(8,128)(2,1)S(1)}, u32[]{:S(2)}, u32[]{:S(2)}) async-start(bf16[64,20,320]{2,1,0:T(8,128)(2,1)} %reshape.537), calls=%async_computation.3 | async-start | bytes 2359296 | tf_op jit(solution)/shard_map/all_to_all | solution.py:64
  311.6 31.7 %copy-start.1 = (bf16[256,1024]{1,0:T(8,128)(2,1)S(1)}, bf16[256,1024]{1,0:T(8,128)(2,1)}, u32[]{:S(2)}) copy-start(bf16[256,1024]{1,0:T(8,128)(2,1)} %param.11) | copy-start | bytes 1572868
Sparse Core Ops, SparseCore 0:
  38.9 73.3 all-gather.5
  115.4 86.6 all-gather.7
  220.5 35.3 reduce-scatter.1
  258.1 29.1 all-gather.9
